TPU v7x, 128 devices: a whole 4x4x4 slice. The times are simulated.
128 devices in a mesh: rows: 16 (over y, z), feat: 8 (over x, core).
Axes of the slice: x: 4, y: 4, z: 4, core: 2. Of those that a mesh axis runs over, the one named last changes fastest.
Arguments:
- features: bfloat16 [32768, 1024], P('rows', 'feat'), may hold values from -6 to 6
- tiles: bfloat16 [10240, 128, 128], P('rows'), may hold values from -0.078125 to 0.078125
- tile_row: int32 [10240], P('rows'), may hold values from 0 to 15, as said below
- tile_panel: int32 [10240], P('rows'), may hold values from 0 to 15
- tile_slot: int32 [10240], P('rows'), may hold values from 0 to 7
- counts: int32 [16], P('rows'), may hold values from 1 to 640, as said below
- need_list: int32 [16, 16, 8], replicated, may hold values from 0 to 15, as said below
- weight: bfloat16 [1024, 1024], replicated, may hold values from -0.1875 to 0.1875
Outputs:
- activations: bfloat16 [32768, 1024], P(('rows', 'feat'))
Inputs may be any that keep to these rules, and one draw needn't show every extreme that they name: need_list[g, p] holds 8 distinct tile rows of panel p. Within a row group the slots name distinct (tile_row, tile_panel, tile_slot) triples. `counts`: some row group lists exactly 640 tiles.
All inputs are finite; a program needn't handle non-finite values.
Results may differ from a plain program's by a relative error of at most 0.0049.
Values may be sent and summed in bfloat16 or wider, within the bound.
A program may use at most 128 MiB of HBM per device.

v0:
```python
import math
import jax
import jax.numpy as jnp
from jax import lax
from jax.sharding import PartitionSpec as P

TILE = 128
TPP = 16
NEED = 8


def aggregate(source, block_ids, tiles, tile_row, live_slot, shard_width):
    slots = tiles.shape[0]
    per_step = math.gcd(slots, 128)
    steps_count = slots // per_step
    blocks = source.reshape(-1, TILE, shard_width)

    def one_step(total, inputs):
        tile_part, id_part, row_part, live_part = inputs
        fetched = jnp.take(blocks, id_part, axis=0)
        product = jnp.einsum("sij,sjh->sih", tile_part, fetched, preferred_element_type=jnp.float32)
        product = jnp.where(live_part[:, None, None], product, 0.0)
        return (total.at[row_part].add(product), None)

    initial = jnp.zeros((TPP, TILE, shard_width), jnp.float32)
    total, unused = lax.scan(
        one_step,
        initial,
        (
            tiles.reshape(steps_count, per_step, TILE, TILE),
            block_ids.reshape(steps_count, per_step),
            tile_row.reshape(steps_count, per_step),
            live_slot.reshape(steps_count, per_step),
        ),
    )
    return total.reshape(TPP * TILE, shard_width)


def per_device(features, tiles, tile_row, tile_panel, tile_slot, counts, need_list, weight):
    shard_width = features.shape[1]
    groups = lax.axis_size("rows")
    own_group = lax.axis_index("rows")
    live_slot = lax.broadcasted_iota(jnp.int32, tile_row.shape, 0) < counts[0]
    source = lax.all_gather(features, "rows", axis=0, tiled=True)
    own_table = lax.dynamic_index_in_dim(need_list, own_group, 0, keepdims=False).reshape(-1)
    flat_index = tile_panel * NEED + tile_slot
    matches = flat_index[:, None] == lax.broadcasted_iota(jnp.int32, (1, groups * NEED), 1)
    picked = jnp.sum(jnp.where(matches, own_table[None, :], 0), axis=1)
    block_ids = tile_panel * TPP + picked
    summed = aggregate(source, block_ids, tiles, tile_row, live_slot, shard_width)
    rounded = summed.astype(jnp.bfloat16)
    rows_full = lax.all_to_all(rounded, "feat", split_axis=0, concat_axis=1, tiled=True)
    mixed = jnp.dot(rows_full, weight, preferred_element_type=jnp.float32)
    return jnp.maximum(mixed, 0.0).astype(jnp.bfloat16)


def solution(mesh):
    return jax.shard_map(
        per_device,
        mesh=mesh,
        in_specs=(
            P("rows", "feat"),
            P("rows", None, None),
            P("rows"),
            P("rows"),
            P("rows"),
            P("rows"),
            P(),
            P(),
        ),
        out_specs=P(("rows", "feat"), None),
        check_vma=False,
    )
```

profile of v0, /device:TPU:1, one launch (start us, length us, event | category | flops | bytes accessed | tf_op | source)
XLA Modules:
  0.0 267.5 jit_solution(11468187125140343390)
XLA Ops:
  6.5 0.0 copy-start
  6.5 0.0 all-gather.2.cloned.1.call-start
  6.5 0.7 all-gather.2.cloned.1.call-update
  7.3 0.7 constant_dynamic-slice_fusion.2
  8.0 0.1 copy.13
  8.0 0.1 broadcast_in_dim.45
  8.8 0.7 multiply_add_fusion
  9.5 0.3 select_reduce_fusion
  9.8 0.7 add_bitcast_fusion
  10.5 73.1 %all-gather.2.cloned.1.call-done = bf16[32768,128]{1,0:T(8,128)(2,1)} async-done(((bf16[2048,128]{1,0:T(8,128)(2,1)}), bf16[32768,128]{1,0:T(8,128)(2,1)}) %all-gather.2.cloned.1.call-update) | async-done | bytes 8388624 | tf_op jit(solution)/shard_map/all_gather | solution.py:44
  83.6 0.1 broadcast_in_dim.44
  83.7 161.1 %while.10 = (s32[]{:T(128)}, f32[16,128,128]{2,1,0:T(8,128)S(1)}, s32[5,128]{1,0:T(8,128)}, pred[5,128]{1,0:T(8,128)(4,1)S(1)}, bf16[5,128,128,128]{3,2,1,0:T(8,...) while((s32[]{:T(128)}, f32[16,128,128]{2,1,0:T(8,128)S(1)}, ...), condition=%wide.region_3.4_spmd, body=%wide.region_1.3_spmd.sunk | while | flops 543164928 | bytes 50341088 | solution.py:26
  83.7 0.7 fusion.23
  84.4 6.4 %gather_fusion = bf16[128,128,128]{2,1,0:T(8,128)(2,1)} fusion(bf16[256,128,128]{2,1,0:T(8,128)(2,1)} %get-tuple-element.128, s32[1024]{0:T(1024)S(1)} %pad_clamp_fusion.2), kind=kCustom, calls=%fused_computation.clone.1 | custom fusion | bytes 8389120 | tf_op jit(solution)/shard_map/while/body/eval_jaxpr/jit(_take)/gather | solution.py:20
  90.9 8.0 %broadcast_select_fusion.2 = f32[128,128,128]{2,1,0:T(8,128)} fusion(pred[128]{0:T(512)(128)(4,1)S(1)} %dynamic-slice_bitcast_fusion.2, bf16[128,128,128]{2,1,0:T(8,128)(2,1)} %gather_fusion, pred[128]{0:T(512)(128)(4,1)S(1)} %compare_and_fusion.2, bf16[5,128,128,128]{3,2,1,0:T(8,128)(2,1)} %get-tuple-element.126, s32[]{:T(128)} %get-tuple-element.114), kind=kOutput, calls=%fused_computation.4.clone.1 | convolution fusion | flops 541065216 | bytes 16777984 | tf_op jit(solution)/shard_map/while/body/eval_jaxpr/sij,sjh->sih/dot_general | solution.py:21
  98.9 17.0 %scatter_fusion = f32[16,128,128]{2,1,0:T(8,128)S(1)} fusion(f32[16,128,128]{2,1,0:T(8,128)S(1)} %get-tuple-element.115, s32[128]{0:T(128)S(1)} %get-tuple-element.104, f32[128,128,128]{2,1,0:T(8,128)} %broadcast_select_fusion.2), kind=kCustom, calls=%fused_computation.1.clone.1 | custom fusion | flops 2097152 | bytes 25166336 | tf_op jit(solution)/shard_map/while/body/eval_jaxpr/scatter-add | solution.py:23
  115.9 0.7 fusion.23
  116.6 6.4 %gather_fusion = bf16[128,128,128]{2,1,0:T(8,128)(2,1)} fusion(bf16[256,128,128]{2,1,0:T(8,128)(2,1)} %get-tuple-element.128, s32[1024]{0:T(1024)S(1)} %pad_clamp_fusion.2), kind=kCustom, calls=%fused_computation.clone.1 | custom fusion | bytes 8389120 | tf_op jit(solution)/shard_map/while/body/eval_jaxpr/jit(_take)/gather | solution.py:20
  123.1 8.0 %broadcast_select_fusion.2 = f32[128,128,128]{2,1,0:T(8,128)} fusion(pred[128]{0:T(512)(128)(4,1)S(1)} %dynamic-slice_bitcast_fusion.2, bf16[128,128,128]{2,1,0:T(8,128)(2,1)} %gather_fusion, pred[128]{0:T(512)(128)(4,1)S(1)} %compare_and_fusion.2, bf16[5,128,128,128]{3,2,1,0:T(8,128)(2,1)} %get-tuple-element.126, s32[]{:T(128)} %get-tuple-element.114), kind=kOutput, calls=%fused_computation.4.clone.1 | convolution fusion | flops 541065216 | bytes 16777984 | tf_op jit(solution)/shard_map/while/body/eval_jaxpr/sij,sjh->sih/dot_general | solution.py:21
  131.1 17.0 %scatter_fusion = f32[16,128,128]{2,1,0:T(8,128)S(1)} fusion(f32[16,128,128]{2,1,0:T(8,128)S(1)} %get-tuple-element.115, s32[128]{0:T(128)S(1)} %get-tuple-element.104, f32[128,128,128]{2,1,0:T(8,128)} %broadcast_select_fusion.2), kind=kCustom, calls=%fused_computation.1.clone.1 | custom fusion | flops 2097152 | bytes 25166336 | tf_op jit(solution)/shard_map/while/body/eval_jaxpr/scatter-add | solution.py:23
  148.2 0.7 fusion.23
  148.9 6.4 %gather_fusion = bf16[128,128,128]{2,1,0:T(8,128)(2,1)} fusion(bf16[256,128,128]{2,1,0:T(8,128)(2,1)} %get-tuple-element.128, s32[1024]{0:T(1024)S(1)} %pad_clamp_fusion.2), kind=kCustom, calls=%fused_computation.clone.1 | custom fusion | bytes 8389120 | tf_op jit(solution)/shard_map/while/body/eval_jaxpr/jit(_take)/gather | solution.py:20
  155.3 8.0 %broadcast_select_fusion.2 = f32[128,128,128]{2,1,0:T(8,128)} fusion(pred[128]{0:T(512)(128)(4,1)S(1)} %dynamic-slice_bitcast_fusion.2, bf16[128,128,128]{2,1,0:T(8,128)(2,1)} %gather_fusion, pred[128]{0:T(512)(128)(4,1)S(1)} %compare_and_fusion.2, bf16[5,128,128,128]{3,2,1,0:T(8,128)(2,1)} %get-tuple-element.126, s32[]{:T(128)} %get-tuple-element.114), kind=kOutput, calls=%fused_computation.4.clone.1 | convolution fusion | flops 541065216 | bytes 16777984 | tf_op jit(solution)/shard_map/while/body/eval_jaxpr/sij,sjh->sih/dot_general | solution.py:21
  163.3 17.0 %scatter_fusion = f32[16,128,128]{2,1,0:T(8,128)S(1)} fusion(f32[16,128,128]{2,1,0:T(8,128)S(1)} %get-tuple-element.115, s32[128]{0:T(128)S(1)} %get-tuple-element.104, f32[128,128,128]{2,1,0:T(8,128)} %broadcast_select_fusion.2), kind=kCustom, calls=%fused_computation.1.clone.1 | custom fusion | flops 2097152 | bytes 25166336 | tf_op jit(solution)/shard_map/while/body/eval_jaxpr/scatter-add | solution.py:23
  180.4 0.7 fusion.23
  181.1 6.4 %gather_fusion = bf16[128,128,128]{2,1,0:T(8,128)(2,1)} fusion(bf16[256,128,128]{2,1,0:T(8,128)(2,1)} %get-tuple-element.128, s32[1024]{0:T(1024)S(1)} %pad_clamp_fusion.2), kind=kCustom, calls=%fused_computation.clone.1 | custom fusion | bytes 8389120 | tf_op jit(solution)/shard_map/while/body/eval_jaxpr/jit(_take)/gather | solution.py:20
  187.5 8.0 %broadcast_select_fusion.2 = f32[128,128,128]{2,1,0:T(8,128)} fusion(pred[128]{0:T(512)(128)(4,1)S(1)} %dynamic-slice_bitcast_fusion.2, bf16[128,128,128]{2,1,0:T(8,128)(2,1)} %gather_fusion, pred[128]{0:T(512)(128)(4,1)S(1)} %compare_and_fusion.2, bf16[5,128,128,128]{3,2,1,0:T(8,128)(2,1)} %get-tuple-element.126, s32[]{:T(128)} %get-tuple-element.114), kind=kOutput, calls=%fused_computation.4.clone.1 | convolution fusion | flops 541065216 | bytes 16777984 | tf_op jit(solution)/shard_map/while/body/eval_jaxpr/sij,sjh->sih/dot_general | solution.py:21
  195.5 17.0 %scatter_fusion = f32[16,128,128]{2,1,0:T(8,128)S(1)} fusion(f32[16,128,128]{2,1,0:T(8,128)S(1)} %get-tuple-element.115, s32[128]{0:T(128)S(1)} %get-tuple-element.104, f32[128,128,128]{2,1,0:T(8,128)} %broadcast_select_fusion.2), kind=kCustom, calls=%fused_computation.1.clone.1 | custom fusion | flops 2097152 | bytes 25166336 | tf_op jit(solution)/shard_map/while/body/eval_jaxpr/scatter-add | solution.py:23
  212.6 0.7 fusion.23
  213.3 6.4 %gather_fusion = bf16[128,128,128]{2,1,0:T(8,128)(2,1)} fusion(bf16[256,128,128]{2,1,0:T(8,128)(2,1)} %get-tuple-element.128, s32[1024]{0:T(1024)S(1)} %pad_clamp_fusion.2), kind=kCustom, calls=%fused_computation.clone.1 | custom fusion | bytes 8389120 | tf_op jit(solution)/shard_map/while/body/eval_jaxpr/jit(_take)/gather | solution.py:20
  219.7 8.0 %broadcast_select_fusion.2 = f32[128,128,128]{2,1,0:T(8,128)} fusion(pred[128]{0:T(512)(128)(4,1)S(1)} %dynamic-slice_bitcast_fusion.2, bf16[128,128,128]{2,1,0:T(8,128)(2,1)} %gather_fusion, pred[128]{0:T(512)(128)(4,1)S(1)} %compare_and_fusion.2, bf16[5,128,128,128]{3,2,1,0:T(8,128)(2,1)} %get-tuple-element.126, s32[]{:T(128)} %get-tuple-element.114), kind=kOutput, calls=%fused_computation.4.clone.1 | convolution fusion | flops 541065216 | bytes 16777984 | tf_op jit(solution)/shard_map/while/body/eval_jaxpr/sij,sjh->sih/dot_general | solution.py:21
  227.7 17.0 %scatter_fusion = f32[16,128,128]{2,1,0:T(8,128)S(1)} fusion(f32[16,128,128]{2,1,0:T(8,128)S(1)} %get-tuple-element.115, s32[128]{0:T(128)S(1)} %get-tuple-element.104, f32[128,128,128]{2,1,0:T(8,128)} %broadcast_select_fusion.2), kind=kCustom, calls=%fused_computation.1.clone.1 | custom fusion | flops 2097152 | bytes 25166336 | tf_op jit(solution)/shard_map/while/body/eval_jaxpr/scatter-add | solution.py:23
  244.8 0.1 convert_element_type.10
  244.9 14.1 %all_to_all.16 = bf16[8,256,128]{2,1,0:T(8,128)(2,1)S(1)} all-to-all(bf16[8,256,128]{2,1,0:T(8,128)(2,1)S(1)} %bitcast.45), channel_id=1, replica_groups=mesh['rows'=16,'feat'=8] {'feat'}, dimensions={0} | all-to-all | bytes 1048576 | tf_op jit(solution)/shard_map/all_to_all | solution.py:52
  259.0 0.2 copy.14
  259.2 0.0 copy-done
  259.2 1.5 fusion.15
  (16 shorter events, 0.2 us)
Async XLA Ops:
  6.5 252.6 %copy-start = (bf16[1024,1024]{1,0:T(8,128)(2,1)S(1)}, bf16[1024,1024]{1,0:T(8,128)(2,1)}, u32[]{:S(2)}) copy-start(bf16[1024,1024]{1,0:T(8,128)(2,1)} %param.17) | copy-start | bytes 6291460
  6.5 77.1 %all-gather.2.cloned.1.call-start = ((), (), s32[]{:S(2)}) async-start(), calls=%async_computation.1 | async-start | bytes 8912896 | tf_op jit(solution)/shard_map/all_gather | solution.py:44
Sparse Core Ops, SparseCore 0:
  9.5 74.0 all-gather.1
where the time goes:
time: 270 us; the launch traced here: 268 us
  other arithmetic  90.5 us (34%)
  waiting for transfers between devices  73.9 us (27%)
  matrix products  41.6 us (15%)
  local copies, waits for them, and re-layouts  33.2 us (12%)
  blocking collectives  14.1 us (5%)
  between operations  14.1 us (5%)
    scatter-add x5, other arithmetic, one_step(): return (total.at[row_part].add(product), None)  85.2 us
    all_gather x1, waiting for transfers between devices, per_device(): source = lax.all_gather(features, 'rows', axis=0, tiled=True)  73.1 us
    dot_general x5, matrix products, one_step(): jnp.einsum('sij,sjh->sih', tile_part, fetched, preferred_element_type=jnp...  40.1 us
    gather x5, local copies, waits for them, and re-layouts, one_step(): fetched = jnp.take(blocks, id_part, axis=0)  32 us
    all_to_all x1, blocking collectives, per_device(): lax.all_to_all(rounded, 'feat', split_axis=0, concat_axis=1, tiled=True)  14.1 us
  transfers between devices with their start and end apart: 1, of which 1 were waited for; matrix products, arithmetic and copies ran while one was open for 1% of the time, Pallas kernels for 0%

commit v1 on v0

--- a/solution.py
+++ b/solution.py
@@ -41,7 +41,10 @@
     groups = lax.axis_size("rows")
     own_group = lax.axis_index("rows")
     live_slot = lax.broadcasted_iota(jnp.int32, tile_row.shape, 0) < counts[0]
-    source = lax.all_gather(features, "rows", axis=0, tiled=True)
+    size = lax.axis_size("rows")
+    pieces = jnp.stack([features for _ in range(size)])
+    pieces = lax.all_to_all(pieces, "rows", split_axis=0, concat_axis=0)
+    source = jnp.concatenate(pieces, axis=0)
     own_table = lax.dynamic_index_in_dim(need_list, own_group, 0, keepdims=False).reshape(-1)
     flat_index = tile_panel * NEED + tile_slot
     matches = flat_index[:, None] == lax.broadcasted_iota(jnp.int32, (1, groups * NEED), 1)

time: 270 us -> 342 us (1.27)
  waiting for transfers between devices: 73.9 us -> 144 us
  between operations: 14.1 us -> 0.75 us
  starting transfers between devices: 0.01 us -> 8.78 us
  local copies, waits for them, and re-layouts: 33.2 us -> 39.2 us
    all_to_all x0 -> x1, waiting for transfers between devices: none -> 144 us  [per_device(): pieces = lax.all_to_all(pieces, 'rows', split_axis=0, concat_axis=0)]
    all_gather x1 -> x0, waiting for transfers between devices: 73.1 us -> none  [per_device(): source = lax.all_gather(features, 'rows', axis=0, tiled=True)]
    all_to_all x0 -> x1, starting transfers between devices: none -> 8.78 us  [per_device(): pieces = lax.all_to_all(pieces, 'rows', split_axis=0, concat_axis=0)]
    another operation x0 -> x1, local copies, waits for them, and re-layouts: none -> 6.02 us  [per_device(): pieces = jnp.stack([features for _ in range(size)])]
  transfers between devices with their start and end apart: 1 -> 1, of which waited for: 1 -> 1; matrix products, arithmetic and copies ran while one was open for 1% -> 0% of each run, Pallas kernels for 0% -> 0%
where the time goes in v1:
time: 342 us; the launch traced here: 340 us
  waiting for transfers between devices  144 us (42%)
  other arithmetic  89.1 us (26%)
  matrix products  41.6 us (12%)
  local copies, waits for them, and re-layouts  39.2 us (11%)
  blocking collectives  15.9 us (5%)
  starting transfers between devices  8.78 us (3%)
    all_to_all x1, waiting for transfers between devices, per_device(): pieces = lax.all_to_all(pieces, 'rows', split_axis=0, concat_axis=0)  144 us
    scatter-add x5, other arithmetic, one_step(): return (total.at[row_part].add(product), None)  85.2 us
    dot_general x5, matrix products, one_step(): jnp.einsum('sij,sjh->sih', tile_part, fetched, preferred_element_type=jnp...  40.1 us
    gather x5, local copies, waits for them, and re-layouts, one_step(): fetched = jnp.take(blocks, id_part, axis=0)  32 us
    all_to_all x1, blocking collectives, per_device(): lax.all_to_all(rounded, 'feat', split_axis=0, concat_axis=1, tiled=True)  15.9 us
    all_to_all x1, starting transfers between devices, per_device(): pieces = lax.all_to_all(pieces, 'rows', split_axis=0, concat_axis=0)  8.78 us
  transfers between devices with their start and end apart: 1, of which 1 were waited for; matrix products, arithmetic and copies ran while one was open for 0% of the time, Pallas kernels for 0%

profile of v1, /device:TPU:1, one launch (start us, length us, event | category | flops | bytes accessed | tf_op | source)
XLA Modules:
  0.0 339.9 jit_solution(7895871420069625294)
XLA Ops:
  0.0 0.0 copy-start
  0.0 6.0 %stack.2 = bf16[16,2048,128]{2,1,0:T(8,128)(2,1)} broadcast(bf16[2048,128]{1,0:T(8,128)(2,1)} %param.10), dimensions={1,2} | broadcast | bytes 8912896 | tf_op jit(solution)/shard_map/stack | solution.py:45
  6.0 0.0 copy-start.1
  6.0 0.0 copy-start.2
  6.0 8.8 %all-to-all-start = ((bf16[16,2048,128]{2,1,0:T(8,128)(2,1)}), bf16[16,2048,128]{2,1,0:T(8,128)(2,1)}, u32[]{:S(2)}, u32[]{:S(2)}) async-start(bf16[16,2048,128]{2,1,0:T(8,128)(2,1)} %stack.2), calls=%async_computation | async-start | bytes 16777216 | tf_op jit(solution)/shard_map/all_to_all | solution.py:46
  14.8 0.7 constant_dynamic-slice_fusion.2
  15.5 0.1 copy.13
  15.6 0.1 broadcast_in_dim.45
  16.3 0.0 copy-done.1
  16.4 0.0 copy-done.2
  16.4 0.3 select_reduce_fusion
  16.7 144.3 %all-to-all-done = bf16[16,2048,128]{2,1,0:T(8,128)(2,1)} async-done(((bf16[16,2048,128]{2,1,0:T(8,128)(2,1)}), bf16[16,2048,128]{2,1,0:T(8,128)(2,1)}, u32[]{:S(2)}, u32[]{:S(2)}) %all-to-all-start) | async-done | bytes 8388640 | tf_op jit(solution)/shard_map/all_to_all | solution.py:46
  161.0 0.1 broadcast_in_dim.44
  161.1 161.1 %while.10 = (s32[]{:T(128)}, f32[16,128,128]{2,1,0:T(8,128)S(1)}, s32[5,128]{1,0:T(8,128)}, pred[5,128]{1,0:T(8,128)(4,1)S(1)}, bf16[5,128,128,128]{3,2,1,0:T(8,...) while((s32[]{:T(128)}, f32[16,128,128]{2,1,0:T(8,128)S(1)}, ...), condition=%wide.region_3.4_spmd, body=%wide.region_1.3_spmd.sunk | while | flops 543164928 | bytes 50341088 | solution.py:26
  161.1 0.7 fusion.23
  161.8 6.4 %gather_fusion = bf16[128,128,128]{2,1,0:T(8,128)(2,1)} fusion(bf16[256,128,128]{2,1,0:T(8,128)(2,1)} %get-tuple-element.128, s32[1024]{0:T(1024)S(1)} %pad_clamp_fusion.2), kind=kCustom, calls=%fused_computation.clone.1 | custom fusion | bytes 8389120 | tf_op jit(solution)/shard_map/while/body/eval_jaxpr/jit(_take)/gather | solution.py:20
  168.2 8.0 %broadcast_select_fusion.2 = f32[128,128,128]{2,1,0:T(8,128)} fusion(pred[128]{0:T(512)(128)(4,1)S(1)} %dynamic-slice_bitcast_fusion.2, bf16[128,128,128]{2,1,0:T(8,128)(2,1)} %gather_fusion, pred[128]{0:T(512)(128)(4,1)S(1)} %compare_and_fusion.2, bf16[5,128,128,128]{3,2,1,0:T(8,128)(2,1)} %get-tuple-element.126, s32[]{:T(128)} %get-tuple-element.114), kind=kOutput, calls=%fused_computation.4.clone.1 | convolution fusion | flops 541065216 | bytes 16777984 | tf_op jit(solution)/shard_map/while/body/eval_jaxpr/sij,sjh->sih/dot_general | solution.py:21
  176.2 17.0 %scatter_fusion = f32[16,128,128]{2,1,0:T(8,128)S(1)} fusion(f32[16,128,128]{2,1,0:T(8,128)S(1)} %get-tuple-element.115, s32[128]{0:T(128)S(1)} %get-tuple-element.104, f32[128,128,128]{2,1,0:T(8,128)} %broadcast_select_fusion.2), kind=kCustom, calls=%fused_computation.1.clone.1 | custom fusion | flops 2097152 | bytes 25166336 | tf_op jit(solution)/shard_map/while/body/eval_jaxpr/scatter-add | solution.py:23
  193.3 0.7 fusion.23
  194.0 6.4 %gather_fusion = bf16[128,128,128]{2,1,0:T(8,128)(2,1)} fusion(bf16[256,128,128]{2,1,0:T(8,128)(2,1)} %get-tuple-element.128, s32[1024]{0:T(1024)S(1)} %pad_clamp_fusion.2), kind=kCustom, calls=%fused_computation.clone.1 | custom fusion | bytes 8389120 | tf_op jit(solution)/shard_map/while/body/eval_jaxpr/jit(_take)/gather | solution.py:20
  200.4 8.0 %broadcast_select_fusion.2 = f32[128,128,128]{2,1,0:T(8,128)} fusion(pred[128]{0:T(512)(128)(4,1)S(1)} %dynamic-slice_bitcast_fusion.2, bf16[128,128,128]{2,1,0:T(8,128)(2,1)} %gather_fusion, pred[128]{0:T(512)(128)(4,1)S(1)} %compare_and_fusion.2, bf16[5,128,128,128]{3,2,1,0:T(8,128)(2,1)} %get-tuple-element.126, s32[]{:T(128)} %get-tuple-element.114), kind=kOutput, calls=%fused_computation.4.clone.1 | convolution fusion | flops 541065216 | bytes 16777984 | tf_op jit(solution)/shard_map/while/body/eval_jaxpr/sij,sjh->sih/dot_general | solution.py:21
  208.4 17.0 %scatter_fusion = f32[16,128,128]{2,1,0:T(8,128)S(1)} fusion(f32[16,128,128]{2,1,0:T(8,128)S(1)} %get-tuple-element.115, s32[128]{0:T(128)S(1)} %get-tuple-element.104, f32[128,128,128]{2,1,0:T(8,128)} %broadcast_select_fusion.2), kind=kCustom, calls=%fused_computation.1.clone.1 | custom fusion | flops 2097152 | bytes 25166336 | tf_op jit(solution)/shard_map/while/body/eval_jaxpr/scatter-add | solution.py:23
  225.5 0.7 fusion.23
  226.2 6.4 %gather_fusion = bf16[128,128,128]{2,1,0:T(8,128)(2,1)} fusion(bf16[256,128,128]{2,1,0:T(8,128)(2,1)} %get-tuple-element.128, s32[1024]{0:T(1024)S(1)} %pad_clamp_fusion.2), kind=kCustom, calls=%fused_computation.clone.1 | custom fusion | bytes 8389120 | tf_op jit(solution)/shard_map/while/body/eval_jaxpr/jit(_take)/gather | solution.py:20
  232.6 8.0 %broadcast_select_fusion.2 = f32[128,128,128]{2,1,0:T(8,128)} fusion(pred[128]{0:T(512)(128)(4,1)S(1)} %dynamic-slice_bitcast_fusion.2, bf16[128,128,128]{2,1,0:T(8,128)(2,1)} %gather_fusion, pred[128]{0:T(512)(128)(4,1)S(1)} %compare_and_fusion.2, bf16[5,128,128,128]{3,2,1,0:T(8,128)(2,1)} %get-tuple-element.126, s32[]{:T(128)} %get-tuple-element.114), kind=kOutput, calls=%fused_computation.4.clone.1 | convolution fusion | flops 541065216 | bytes 16777984 | tf_op jit(solution)/shard_map/while/body/eval_jaxpr/sij,sjh->sih/dot_general | solution.py:21
  240.7 17.0 %scatter_fusion = f32[16,128,128]{2,1,0:T(8,128)S(1)} fusion(f32[16,128,128]{2,1,0:T(8,128)S(1)} %get-tuple-element.115, s32[128]{0:T(128)S(1)} %get-tuple-element.104, f32[128,128,128]{2,1,0:T(8,128)} %broadcast_select_fusion.2), kind=kCustom, calls=%fused_computation.1.clone.1 | custom fusion | flops 2097152 | bytes 25166336 | tf_op jit(solution)/shard_map/while/body/eval_jaxpr/scatter-add | solution.py:23
  257.7 0.7 fusion.23
  258.4 6.4 %gather_fusion = bf16[128,128,128]{2,1,0:T(8,128)(2,1)} fusion(bf16[256,128,128]{2,1,0:T(8,128)(2,1)} %get-tuple-element.128, s32[1024]{0:T(1024)S(1)} %pad_clamp_fusion.2), kind=kCustom, calls=%fused_computation.clone.1 | custom fusion | bytes 8389120 | tf_op jit(solution)/shard_map/while/body/eval_jaxpr/jit(_take)/gather | solution.py:20
  264.8 8.0 %broadcast_select_fusion.2 = f32[128,128,128]{2,1,0:T(8,128)} fusion(pred[128]{0:T(512)(128)(4,1)S(1)} %dynamic-slice_bitcast_fusion.2, bf16[128,128,128]{2,1,0:T(8,128)(2,1)} %gather_fusion, pred[128]{0:T(512)(128)(4,1)S(1)} %compare_and_fusion.2, bf16[5,128,128,128]{3,2,1,0:T(8,128)(2,1)} %get-tuple-element.126, s32[]{:T(128)} %get-tuple-element.114), kind=kOutput, calls=%fused_computation.4.clone.1 | convolution fusion | flops 541065216 | bytes 16777984 | tf_op jit(solution)/shard_map/while/body/eval_jaxpr/sij,sjh->sih/dot_general | solution.py:21
  272.9 17.0 %scatter_fusion = f32[16,128,128]{2,1,0:T(8,128)S(1)} fusion(f32[16,128,128]{2,1,0:T(8,128)S(1)} %get-tuple-element.115, s32[128]{0:T(128)S(1)} %get-tuple-element.104, f32[128,128,128]{2,1,0:T(8,128)} %broadcast_select_fusion.2), kind=kCustom, calls=%fused_computation.1.clone.1 | custom fusion | flops 2097152 | bytes 25166336 | tf_op jit(solution)/shard_map/while/body/eval_jaxpr/scatter-add | solution.py:23
  289.9 0.7 fusion.23
  290.6 6.4 %gather_fusion = bf16[128,128,128]{2,1,0:T(8,128)(2,1)} fusion(bf16[256,128,128]{2,1,0:T(8,128)(2,1)} %get-tuple-element.128, s32[1024]{0:T(1024)S(1)} %pad_clamp_fusion.2), kind=kCustom, calls=%fused_computation.clone.1 | custom fusion | bytes 8389120 | tf_op jit(solution)/shard_map/while/body/eval_jaxpr/jit(_take)/gather | solution.py:20
  297.0 8.0 %broadcast_select_fusion.2 = f32[128,128,128]{2,1,0:T(8,128)} fusion(pred[128]{0:T(512)(128)(4,1)S(1)} %dynamic-slice_bitcast_fusion.2, bf16[128,128,128]{2,1,0:T(8,128)(2,1)} %gather_fusion, pred[128]{0:T(512)(128)(4,1)S(1)} %compare_and_fusion.2, bf16[5,128,128,128]{3,2,1,0:T(8,128)(2,1)} %get-tuple-element.126, s32[]{:T(128)} %get-tuple-element.114), kind=kOutput, calls=%fused_computation.4.clone.1 | convolution fusion | flops 541065216 | bytes 16777984 | tf_op jit(solution)/shard_map/while/body/eval_jaxpr/sij,sjh->sih/dot_general | solution.py:21
  305.1 17.0 %scatter_fusion = f32[16,128,128]{2,1,0:T(8,128)S(1)} fusion(f32[16,128,128]{2,1,0:T(8,128)S(1)} %get-tuple-element.115, s32[128]{0:T(128)S(1)} %get-tuple-element.104, f32[128,128,128]{2,1,0:T(8,128)} %broadcast_select_fusion.2), kind=kCustom, calls=%fused_computation.1.clone.1 | custom fusion | flops 2097152 | bytes 25166336 | tf_op jit(solution)/shard_map/while/body/eval_jaxpr/scatter-add | solution.py:23
  322.1 0.1 convert_element_type.10
  322.2 15.9 %all_to_all.21 = bf16[8,256,128]{2,1,0:T(8,128)(2,1)S(1)} all-to-all(bf16[8,256,128]{2,1,0:T(8,128)(2,1)S(1)} %bitcast.44), channel_id=1, replica_groups=mesh['rows'=16,'feat'=8] {'feat'}, dimensions={0} | all-to-all | bytes 1048576 | tf_op jit(solution)/shard_map/all_to_all | solution.py:55
  338.1 0.2 copy.14
  338.4 0.0 copy-done
  338.4 1.5 fusion.15
  (18 shorter events, 0.2 us)
Async XLA Ops:
  0.0 338.4 %copy-start = (bf16[1024,1024]{1,0:T(8,128)(2,1)S(1)}, bf16[1024,1024]{1,0:T(8,128)(2,1)}, u32[]{:S(2)}) copy-start(bf16[1024,1024]{1,0:T(8,128)(2,1)} %param.17) | copy-start | bytes 6291460
  6.0 10.3 %copy-start.1 = (s32[640]{0:T(1024)S(1)}, s32[640]{0:T(1024)}, u32[]{:S(2)}) copy-start(s32[640]{0:T(1024)} %param.13) | copy-start | bytes 7684
  6.0 10.3 %copy-start.2 = (s32[640]{0:T(1024)S(1)}, s32[640]{0:T(1024)}, u32[]{:S(2)}) copy-start(s32[640]{0:T(1024)} %param.14) | copy-start | bytes 7684
  6.0 154.9 %all-to-all-start = ((bf16[16,2048,128]{2,1,0:T(8,128)(2,1)}), bf16[16,2048,128]{2,1,0:T(8,128)(2,1)}, u32[]{:S(2)}, u32[]{:S(2)}) async-start(bf16[16,2048,128]{2,1,0:T(8,128)(2,1)} %stack.2), calls=%async_computation | async-start | bytes 16777216 | tf_op jit(solution)/shard_map/all_to_all | solution.py:46
